TPU v7x, 512 devices: a whole 4x8x8 slice. The times are simulated.
512 devices in a mesh: row: 16 (over x, y_lo, core), col: 32 (over y_hi, z).
Axes of the slice: x: 4, y: 8 (y_hi: 4, y_lo: 2; y = y_hi * 2 + y_lo), z: 8, core: 2. Of those that a mesh axis runs over, the one named last changes fastest.
Arguments:
- iterate: bfloat16 [4096, 18432], P('row', 'col'), may hold values from -0.03125 to 0.03125
Outputs:
- update: bfloat16 [4096, 18432], P('row', 'col')
All inputs are finite; a program needn't handle non-finite values.
Results may differ from a plain program's by a relative error of at most 0.006.
Values may be sent and summed in bfloat16 or wider, within the bound.
No kernel may reach another device: no remote copies, remote signals or barrier semaphores. Data moves between devices by JAX's collectives and lax.ppermute only.
A program may use at most 64 MiB of HBM per device.

v0:
```python
import math

import jax
import jax.numpy as jnp
from jax import lax
from jax.sharding import PartitionSpec as P

coef_linear = 3.4445
coef_cubic = -4.775
coef_quintic = 2.0315


def on_device(iterate):
    rows_dev, cols_dev = iterate.shape
    total_rows = rows_dev * lax.axis_size("row")
    total_cols = cols_dev * lax.axis_size("col")
    gathered = lax.all_gather(iterate, "row", axis=0, tiled=True)
    gram_tile = lax.psum_scatter(
        lax.dot_general(
            gathered, iterate, (((1,), (1,)), ((), ())), preferred_element_type=jnp.float32
        ),
        "col",
        scatter_dimension=0,
        tiled=True,
    ).astype(jnp.bfloat16)
    gram_band = lax.all_gather(gram_tile, "row", axis=1, tiled=True)
    matching = gram_band
    squared = jnp.dot(
        matching,
        lax.all_gather(gram_tile, "col", axis=0, tiled=True),
        preferred_element_type=jnp.float32,
    )
    mixed_tile = (coef_cubic * gram_tile.astype(jnp.float32) + coef_quintic * squared).astype(
        jnp.bfloat16
    )
    matching = gathered
    product = lax.dot_general(
        lax.all_gather(mixed_tile, "col", axis=0, tiled=True),
        matching,
        (((0,), (0,)), ((), ())),
        preferred_element_type=jnp.float32,
    )
    update_scale = 0.2 * math.sqrt(max(total_rows, total_cols))
    update = update_scale * (coef_linear * iterate.astype(jnp.float32) + product)
    return update.astype(jnp.bfloat16)


def solution(mesh):
    return jax.shard_map(
        on_device,
        mesh=mesh,
        in_specs=(P("row", "col"),),
        out_specs=P("row", "col"),
        check_vma=False,
    )
```

profile of v0, /device:TPU:1, one launch (start us, length us, event | category | flops | bytes accessed | tf_op | source)
XLA Modules:
  0.0 529.6 jit_solution(10287782727322354203)
XLA Ops:
  6.5 0.0 all-gather.5.cloned.1.call-start
  6.5 0.7 all-gather.5.cloned.1.call-update
  7.3 0.0 reduce-scatter.2.cloned.1.call-start
  7.3 62.4 %all-gather.5.cloned.1.call-done = bf16[4096,576]{0,1:T(8,128)(2,1)} async-done(((bf16[256,576]{0,1:T(8,128)(2,1)}), bf16[4096,576]{0,1:T(8,128)(2,1)}) %all-gather.5.cloned.1.call-update) | async-done | bytes 4718608 | tf_op jit(solution)/shard_map/all_gather | solution.py:17
  69.7 6.3 %fusion.4 = f32[4096,256]{1,0:T(8,128)} fusion(bf16[4096,576]{0,1:T(8,128)(2,1)} %all-gather.5.cloned.1.call-done, bf16[256,576]{0,1:T(8,128)(2,1)} %param.1), kind=kOutput, calls=%fused_computation.6 | convolution fusion | flops 1207959552 | bytes 9207808 | tf_op jit(solution)/shard_map/dot_general | solution.py:19
  76.0 0.0 copy-start
  76.0 0.0 reduce-scatter.2.cloned.1.call-update
  76.0 0.0 all-gather.7.cloned.1.call-start
  76.1 225.5 %reduce-scatter.2.cloned.1.call-done = f32[128,256]{1,0:T(8,128)} async-done(((f32[4096,256]{1,0:T(8,128)}), f32[128,256]{1,0:T(8,128)}) %reduce-scatter.2.cloned.1.call-update) | async-done | bytes 131088 | tf_op jit(solution)/shard_map/reduce_scatter | solution.py:18
  301.6 1.5 convert_element_type.16
  303.1 0.0 all-gather.7.cloned.1.call-update
  303.2 0.0 all-gather.9.cloned.1.call-start
  303.2 0.5 all-gather.9.cloned.1.call-update
  303.7 0.0 all-gather.11.cloned.1.call-start
  303.8 40.9 %all-gather.7.cloned.1.call-done = bf16[128,4096]{1,0:T(8,128)(2,1)} async-done(((bf16[128,256]{1,0:T(8,128)(2,1)}), bf16[128,4096]{1,0:T(8,128)(2,1)}) %all-gather.7.cloned.1.call-update) | async-done | bytes 1048592 | tf_op jit(solution)/shard_map/all_gather | solution.py:26
  344.7 87.5 %all-gather.9.cloned.1.call-done = bf16[4096,256]{1,0:T(8,128)(2,1)} async-done(((bf16[128,256]{1,0:T(8,128)(2,1)}), bf16[4096,256]{1,0:T(8,128)(2,1)}) %all-gather.9.cloned.1.call-update) | async-done | bytes 2097168 | tf_op jit(solution)/shard_map/all_gather | solution.py:30
  432.1 2.9 fusion.3
  435.1 0.0 all-gather.11.cloned.1.call-update
  435.1 82.8 %all-gather.11.cloned.1.call-done = bf16[4096,256]{1,0:T(8,128)(2,1)} async-done(((bf16[128,256]{1,0:T(8,128)(2,1)}), bf16[4096,256]{1,0:T(8,128)(2,1)}) %all-gather.11.cloned.1.call-update) | async-done | bytes 2097168 | tf_op jit(solution)/shard_map/all_gather | solution.py:38
  517.9 0.0 copy-done
  517.9 5.1 fusion.1
Async XLA Ops:
  6.5 63.2 %all-gather.5.cloned.1.call-start = ((), (), s32[]{:S(2)}) async-start(), calls=%async_computation.1 | async-start | bytes 5013504 | tf_op jit(solution)/shard_map/all_gather | solution.py:17
  7.3 294.3 %reduce-scatter.2.cloned.1.call-start = ((), (), s32[]{:S(2)}) async-start(), calls=%async_computation.2 | async-start | bytes 4325376 | tf_op jit(solution)/shard_map/reduce_scatter | solution.py:18
  76.0 441.9 %copy-start = (bf16[256,576]{0,1:T(8,128)(2,1)S(1)}, bf16[256,576]{0,1:T(8,128)(2,1)}, u32[]{:S(2)}) copy-start(bf16[256,576]{0,1:T(8,128)(2,1)} %param.1) | copy-start | bytes 884740
  76.0 268.7 %all-gather.7.cloned.1.call-start = ((), (), s32[]{:S(2)}) async-start(), calls=%async_computation.3 | async-start | bytes 1114112 | tf_op jit(solution)/shard_map/all_gather | solution.py:26
  303.2 129.0 %all-gather.9.cloned.1.call-start = ((), (), s32[]{:S(2)}) async-start(), calls=%async_computation.4 | async-start | bytes 2162688 | tf_op jit(solution)/shard_map/all_gather | solution.py:30
  303.7 214.2 %all-gather.11.cloned.1.call-start = ((), (), s32[]{:S(2)}) async-start(), calls=%async_computation.5 | async-start | bytes 2162688 | tf_op jit(solution)/shard_map/all_gather | solution.py:38
Sparse Core Ops, SparseCore 0:
  9.4 60.2 all-gather.4
  76.1 225.4 reduce-scatter.1
  303.9 40.7 all-gather.6
  348.2 83.9 all-gather.8
  435.6 82.2 all-gather.10
where the time goes:
time: 531 us; the launch traced here: 530 us
  waiting for transfers between devices  500 us (94%)
  matrix products  14.3 us (3%)
  between operations  13.1 us (2%)
    reduce_scatter x1, waiting for transfers between devices, on_device(): lax.psum_scatter(lax.dot_general(gathered, iterate, (((1,), (1,)), ((), (...  226 us
    all_gather x1, waiting for transfers between devices, on_device(): lax.all_gather(gram_tile, 'col', axis=0, tiled=True)  87.5 us
    all_gather x1, waiting for transfers between devices, on_device(): lax.all_gather(mixed_tile, 'col', axis=0, tiled=True)  82.8 us
    all_gather x1, waiting for transfers between devices, on_device(): gathered = lax.all_gather(iterate, 'row', axis=0, tiled=True)  62.4 us
    all_gather x1, waiting for transfers between devices, on_device(): gram_band = lax.all_gather(gram_tile, 'row', axis=1, tiled=True)  40.9 us
  transfers between devices with their start and end apart: 5, of which 5 were waited for; matrix products, arithmetic and copies ran while one was open for 0% of the time, Pallas kernels for 0%

commit v1 on v0

v1 whole, which is shorter than its diff:
```python
import math

import jax
import jax.numpy as jnp
from jax import lax
from jax.experimental import pallas as pl
from jax.experimental.pallas import tpu as pltpu
from jax.sharding import Mesh, PartitionSpec as P

coef_linear = 3.4445
coef_cubic = -4.775
coef_quintic = 2.0315

X, YL, CORE, YH, Z = 4, 2, 2, 4, 8
COL = ("yh", "z")
f32 = jnp.float32
bf16 = jnp.bfloat16

BLOCKS = 9
PIECE = 16


def shift(value, axis, size, by):
    return lax.ppermute(value, axis, [(i, (i + by) % size) for i in range(size)])


def dot(a, b, ca, cb):
    return lax.dot_general(a, b, (((ca,), (cb,)), ((), ())), preferred_element_type=f32)


def gram_kernel(flag, a0m, a0o, a1m, a2m, a2o, a3m, a3o, out):
    f2, f3 = flag[0] == 1, flag[1] == 1
    n = a0m.shape[1]
    a2f = jnp.where(f2, a2o[...], a2m[...])
    a3f = jnp.where(f3, a3o[...], a3m[...])
    pairs = [
        (a1m, a0m), (a1m, a0o), (a1m, a3m), (a1m, a3o),
        (a0m, a2f), (a0m, a3f), (a2m, a3f), (a0m, a0m), (a0m, a0o),
    ]
    for i, (a, b) in enumerate(pairs):
        block = dot(a[...], b[...], 0, 0).astype(bf16)
        for h in range(2):
            half = block[:, h * 128:(h + 1) * 128]
            out[h * 16:(h + 1) * 16, i * PIECE:(i + 1) * PIECE, :] = half.reshape(n // PIECE, PIECE, 128)


def apply_kernel(flag, gm, go, a0m, a0o, a1m, a1o, a2m, a2o, a3m, a3o, o0, o1, o2, o3):
    f2, f3 = flag[0] == 1, flag[1] == 1
    n = a0m.shape[1]

    def block(g, i):
        halves = [
            g[h * 16:(h + 1) * 16, i * PIECE:(i + 1) * PIECE, :].reshape(n, 128) for h in range(2)
        ]
        return jnp.concatenate(halves, axis=1)

    a2f = jnp.where(f2, a2o[...], a2m[...])
    a3f = jnp.where(f3, a3o[...], a3m[...])
    a0f2 = jnp.where(f2, a0o[...], a0m[...])
    a0f3 = jnp.where(f3, a0o[...], a0m[...])
    a2f3 = jnp.where(f3, a2o[...], a2m[...])
    own4, own5, own6 = block(gm, 4), block(gm, 5), block(gm, 6)
    got4 = jnp.where(f2, block(go, 4), own4)
    got5 = jnp.where(f3, block(go, 5), own5)
    got6 = jnp.where(f3, block(go, 6), own6)
    g0, g1, g2, g3 = [block(gm, i) for i in range(4)]
    o0[...] = (
        dot(a0m[...], block(gm, 7), 1, 0)
        + dot(a0o[...], block(gm, 8), 1, 1)
        + dot(a1m[...], g0, 1, 0)
        + dot(a1o[...], block(go, 1), 1, 0)
        + dot(a2f, own4, 1, 1)
        + dot(a3f, own5, 1, 1)
    )
    o1[...] = (
        dot(a0m[...], g0, 1, 1)
        + dot(a0o[...], g1, 1, 1)
        + dot(a3m[...], g2, 1, 1)
        + dot(a3o[...], g3, 1, 1)
    ).astype(bf16)
    o2[...] = (dot(a0f2, got4, 1, 0) + dot(a3f, own6, 1, 1)).astype(bf16)
    o3[...] = (
        dot(a1m[...], g2, 1, 0)
        + dot(a1o[...], block(go, 3), 1, 0)
        + dot(a0f3, got5, 1, 0)
        + dot(a2f3, got6, 1, 0)
    ).astype(bf16)


def call(kernel, outs, ops, flops):
    whole = pl.BlockSpec(memory_space=pltpu.VMEM)
    nbytes = sum(math.prod(v.shape) * v.dtype.itemsize for v in list(outs) + list(ops))
    return pl.pallas_call(
        kernel,
        out_shape=outs,
        in_specs=[pl.BlockSpec(memory_space=pltpu.SMEM)] + [whole] * (len(ops) - 1),
        out_specs=[whole] * len(outs),
        compiler_params=pltpu.CompilerParams(vmem_limit_bytes=24 * 2**20),
        cost_estimate=pl.CostEstimate(flops=flops, bytes_accessed=nbytes, transcendentals=0),
    )(*ops)


def gather(own):
    q1 = shift(own, "x", X, -1)
    q3 = shift(own, "yl", YL, 1)
    q2 = shift(own, "x", X, 2)
    swap = lambda v: shift(v, "core", CORE, 1)
    return [own, swap(own), q1, swap(q1), q2, swap(q2), q3, swap(q3)]


def apply_gram(flag, gm, go, parts):
    k, n = parts[0].shape
    outs = [jax.ShapeDtypeStruct((k, n), f32)] + [jax.ShapeDtypeStruct((k, n), bf16)] * 3
    o0, o1, o2, o3 = call(apply_kernel, outs, [flag, gm, go] + parts, 2 * 16 * k * n * n)
    r1 = shift(o1, "x", X, 1)
    r3 = shift(o3, "yl", YL, 1)
    r2 = shift(o2, "x", X, 2)
    return o0 + (r1.astype(f32) + r3.astype(f32) + r2.astype(f32))


def on_device(iterate):
    own = iterate.T
    k, n = own.shape
    scale = 0.2 * math.sqrt(max(n * X * YL * CORE, k * YH * Z))
    flag = jnp.stack([lax.axis_index("x") // 2, lax.axis_index("yl")]).astype(jnp.int32)
    parts = gather(own)
    a0m, a0o, a1m, a1o, a2m, a2o, a3m, a3o = parts
    shape = jax.ShapeDtypeStruct((YH * Z, BLOCKS * PIECE, 128), bf16)
    pieces = call(gram_kernel, [shape], [flag, a0m, a0o, a1m, a2m, a2o, a3m, a3o], 2 * 9 * k * n * n)[0]
    pieces = lax.all_to_all(pieces, COL, 0, 0)
    tile = pieces.astype(f32).sum(0).astype(bf16)
    gm = lax.all_to_all(jnp.broadcast_to(tile[None], shape.shape), COL, 0, 0)
    go = shift(gm, "core", CORE, 1)
    b = apply_gram(flag, gm, go, parts)
    d = (coef_cubic * own.astype(f32) + coef_quintic * b).astype(bf16)
    c = apply_gram(flag, gm, go, gather(d))
    return (scale * (coef_linear * own.astype(f32) + c)).astype(bf16).T


def solution(mesh):
    fine = Mesh(mesh.devices.reshape(X, YL, CORE, YH, Z), ("x", "yl", "core", "yh", "z"))
    spec = P(("x", "yl", "core"), ("yh", "z"))
    return jax.shard_map(on_device, mesh=fine, in_specs=(spec,), out_specs=spec, check_vma=False)
```

time: 531 us -> 192 us (0.36)
  waiting for transfers between devices: 500 us -> 22.9 us
  blocking collectives: 0 us -> 88.6 us
  starting transfers between devices: 0.16 us -> 70.9 us
  matrix products: 14.3 us -> 0 us
  between operations: 13.1 us -> 0.28 us
  Pallas kernels: 0 us -> 5.59 us
    all_gather x4 -> x0, waiting for transfers between devices: 274 us -> none  [the longest x1 87.5 us: on_device(): lax.all_gather(gram_tile, 'col', axis=0, tiled=True)]
    reduce_scatter x1 -> x0, waiting for transfers between devices: 226 us -> none  [on_device(): lax.psum_scatter(lax.dot_general(gathered, iterate, (((1,), (1,)), ((), (...]
    all_to_all x0 -> x2, blocking collectives: none -> 88.6 us  [the longest x1 44.6 us: on_device(): gm = lax.all_to_all(jnp.broadcast_to(tile[None], shape.shape), COL, 0, 0)]
    ppermute x0 -> x21, starting transfers between devices: none -> 70.9 us  [shift(): lax.ppermute(value, axis, [(i, (i + by) % size) for i in range(size)])]
    ppermute x0 -> x21, waiting for transfers between devices: none -> 22.9 us  [shift(): lax.ppermute(value, axis, [(i, (i + by) % size) for i in range(size)])]
    dot_general x3 -> x0, matrix products: 14.3 us -> none  [the longest x1 6.25 us: on_device(): lax.dot_general(gathered, iterate, (((1,), (1,)), ((), ())), preferred_el...]
    pallas_call x0 -> x3, Pallas kernels: none -> 5.59 us  [call(): pl.pallas_call(kernel, out_shape=outs, in_specs=[pl.BlockSpec(memory_spac...]
  transfers between devices with their start and end apart: 5 -> 21, of which waited for: 5 -> 11; matrix products, arithmetic and copies ran while one was open for 0% -> 0% of each run, Pallas kernels for 0% -> 0%
where the time goes in v1:
time: 192 us; the launch traced here: 191 us
  blocking collectives  88.6 us (46%)
  starting transfers between devices  70.9 us (37%)
  waiting for transfers between devices  22.9 us (12%)
  Pallas kernels  5.59 us (3%)
    ppermute x21, starting transfers between devices, shift(): lax.ppermute(value, axis, [(i, (i + by) % size) for i in range(size)])  70.9 us
    all_to_all x1, blocking collectives, on_device(): gm = lax.all_to_all(jnp.broadcast_to(tile[None], shape.shape), COL, 0, 0)  44.6 us
    all_to_all x1, blocking collectives, on_device(): pieces = lax.all_to_all(pieces, COL, 0, 0)  44.1 us
    ppermute x21, waiting for transfers between devices, shift(): lax.ppermute(value, axis, [(i, (i + by) % size) for i in range(size)])  22.9 us
    pallas_call x3, Pallas kernels, call(): pl.pallas_call(kernel, out_shape=outs, in_specs=[pl.BlockSpec(memory_spac...  5.59 us
  transfers between devices with their start and end apart: 21, of which 11 were waited for; matrix products, arithmetic and copies ran while one was open for 0% of the time, Pallas kernels for 0%

profile of v1, /device:TPU:1, one launch (start us, length us, event | category | flops | bytes accessed | tf_op | source)
XLA Modules:
  0.0 190.8 jit_solution(2699682390596156075)
XLA Ops:
  0.0 4.0 %collective-permute-start.4 = (bf16[576,256]{1,0:T(8,128)(2,1)}, bf16[576,256]{1,0:T(8,128)(2,1)S(1)}, u32[]{:S(2)}, u32[]{:S(2)}) collective-permute-start(bf16[576,256]{1,0:T(8,128)(2,1)} %bitcast.7), channel_id=1, source_target_pairs={{0,64},{64,0},{1,65},{65,1},{2,66},{66,2},{3,67},{67,3},{4,68},{68... | collective-permute-start | bytes 884744 | tf_op jit(solution)/shard_map/ppermute | solution.py:24
  4.0 4.7 %collective-permute-start.2 = (bf16[576,256]{1,0:T(8,128)(2,1)}, bf16[576,256]{1,0:T(8,128)(2,1)S(1)}, u32[]{:S(2)}, u32[]{:S(2)}) collective-permute-start(bf16[576,256]{1,0:T(8,128)(2,1)} %bitcast.8), channel_id=1, source_target_pairs={{0,256},{128,384},{256,0},{384,128},{1,257},{129,385},{257,1},{385... | collective-permute-start | bytes 884744 | tf_op jit(solution)/shard_map/ppermute | solution.py:24
  8.7 2.8 %collective-permute-start.1 = (bf16[576,256]{1,0:T(8,128)(2,1)}, bf16[576,256]{1,0:T(8,128)(2,1)S(1)}, u32[]{:S(2)}, u32[]{:S(2)}) collective-permute-start(bf16[576,256]{1,0:T(8,128)(2,1)} %bitcast.9), channel_id=1, source_target_pairs={{0,384},{128,0},{256,128},{384,256},{1,385},{129,1},{257,129},{385... | collective-permute-start | bytes 884744 | tf_op jit(solution)/shard_map/ppermute | solution.py:24
  11.5 3.4 %collective-permute-start = (bf16[576,256]{1,0:T(8,128)(2,1)}, bf16[576,256]{1,0:T(8,128)(2,1)S(1)}, u32[]{:S(2)}, u32[]{:S(2)}) collective-permute-start(bf16[576,256]{1,0:T(8,128)(2,1)} %bitcast.10), channel_id=1, source_target_pairs={{0,32},{32,0},{1,33},{33,1},{2,34},{34,2},{3,35},{35,3},{4,36},{36... | collective-permute-start | bytes 884744 | tf_op jit(solution)/shard_map/ppermute | solution.py:24
  14.9 2.7 %collective-permute-start.5 = (bf16[576,256]{1,0:T(8,128)(2,1)S(1)}, bf16[576,256]{1,0:T(8,128)(2,1)S(1)}, u32[]{:S(2)}, u32[]{:S(2)}) collective-permute-start(bf16[576,256]{1,0:T(8,128)(2,1)S(1)} %collective-permute-done.4.a3m), channel_id=1, source_target_pairs={{0,32},{32,0},{1,33},{33,1},{2,34},{34,2},{3,35},{35,3},{4,36},{36... | collective-permute-start | bytes 884744 | tf_op jit(solution)/shard_map/ppermute | solution.py:24
  17.6 3.4 %collective-permute-start.3 = (bf16[576,256]{1,0:T(8,128)(2,1)S(1)}, bf16[576,256]{1,0:T(8,128)(2,1)S(1)}, u32[]{:S(2)}, u32[]{:S(2)}) collective-permute-start(bf16[576,256]{1,0:T(8,128)(2,1)S(1)} %collective-permute-done.2.a2m), channel_id=1, source_target_pairs={{0,32},{32,0},{1,33},{33,1},{2,34},{34,2},{3,35},{35,3},{4,36},{36... | collective-permute-start | bytes 884744 | tf_op jit(solution)/shard_map/ppermute | solution.py:24
  23.2 1.7 shard_map.17
  24.9 44.1 %all_to_all.10 = bf16[32,144,128]{2,1,0:T(8,128)(2,1)S(1)} all-to-all(bf16[32,144,128]{2,1,0:T(8,128)(2,1)S(1)} %shard_map.17), channel_id=1, replica_groups=mesh['x'=4,'yl'=2,'core'=2,'yh'=4,'z'=8] {'yh','z'}, dimensions={0} | all-to-all | bytes 2359296 | tf_op jit(solution)/shard_map/all_to_all | solution.py:130
  69.3 44.6 %all_to_all.11.gm = bf16[32,144,128]{2,1,0:T(8,128)(2,1)S(1)} all-to-all(bf16[32,144,128]{2,1,0:T(8,128)(2,1)S(1)} %broadcast_in_dim.2), channel_id=1, replica_groups=mesh['x'=4,'yl'=2,'core'=2,'yh'=4,'z'=8] {'yh','z'}, dimensions={0} | all-to-all | bytes 2359296 | tf_op jit(solution)/shard_map/all_to_all | solution.py:132
  113.9 4.6 %collective-permute-start.6 = (bf16[32,144,128]{2,1,0:T(8,128)(2,1)S(1)}, bf16[32,144,128]{2,1,0:T(8,128)(2,1)S(1)}, u32[]{:S(2)}, u32[]{:S(2)}) collective-permute-start(bf16[32,144,128]{2,1,0:T(8,128)(2,1)S(1)} %all_to_all.11.gm), channel_id=1, source_target_pairs={{0,32},{32,0},{1,33},{33,1},{2,34},{34,2},{3,35},{35,3},{4,36},{36... | collective-permute-start | bytes 3538952 | tf_op jit(solution)/shard_map/ppermute | solution.py:24
  118.5 1.9 %collective-permute-start.7 = (bf16[576,256]{1,0:T(8,128)(2,1)S(1)}, bf16[576,256]{1,0:T(8,128)(2,1)S(1)}, u32[]{:S(2)}, u32[]{:S(2)}) collective-permute-start(bf16[576,256]{1,0:T(8,128)(2,1)S(1)} %collective-permute-done.1.a1m), channel_id=1, source_target_pairs={{0,32},{32,0},{1,33},{33,1},{2,34},{34,2},{3,35},{35,3},{4,36},{36... | collective-permute-start | bytes 884744 | tf_op jit(solution)/shard_map/ppermute | solution.py:24
  120.4 1.5 collective-permute-done.7.a1o
  121.9 2.0 %shard_map.18 = (f32[576,256]{1,0:T(8,128)S(1)}, bf16[576,256]{1,0:T(8,128)(2,1)S(1)}, bf16[576,256]{1,0:T(8,128)(2,1)S(1)}, bf16[576,256]{1,0:T(8,128)(2,1)S(1)}) custom-call(s32[2]{0:T(128)S(1)} %pad_add_fusion.flag, bf16[32,144,128]{2,1,0:T(8,128)(2,1)S(1)} %all_to_all.11.gm, bf16[32,144,128]{2,1,0:T(8,128)(2,1)S(1)} %collective-permute-done.6.go, ...), custom_call_target="tpu_custom_call" | custom-call | flops 1207959552 | bytes 6193160 | tf_op jit(solution)/shard_map/pallas_call | solution.py:93
  123.9 7.1 %collective-permute-start.8 = (bf16[576,256]{1,0:T(8,128)(2,1)S(1)}, bf16[576,256]{1,0:T(8,128)(2,1)S(1)}, u32[]{:S(2)}, u32[]{:S(2)}) collective-permute-start(bf16[576,256]{1,0:T(8,128)(2,1)S(1)} %get-tuple-element.14), channel_id=1, source_target_pairs={{0,128},{128,256},{256,384},{384,0},{1,129},{129,257},{257,385},{3... | collective-permute-start | bytes 884744 | tf_op jit(solution)/shard_map/ppermute | solution.py:24
  131.0 1.9 %collective-permute-start.9 = (bf16[576,256]{1,0:T(8,128)(2,1)S(1)}, bf16[576,256]{1,0:T(8,128)(2,1)S(1)}, u32[]{:S(2)}, u32[]{:S(2)}) collective-permute-start(bf16[576,256]{1,0:T(8,128)(2,1)S(1)} %get-tuple-element.15), channel_id=1, source_target_pairs={{0,64},{64,0},{1,65},{65,1},{2,66},{66,2},{3,67},{67,3},{4,68},{68... | collective-permute-start | bytes 884744 | tf_op jit(solution)/shard_map/ppermute | solution.py:24
  133.0 4.5 %collective-permute-start.10 = (bf16[576,256]{1,0:T(8,128)(2,1)S(1)}, bf16[576,256]{1,0:T(8,128)(2,1)S(1)}, u32[]{:S(2)}, u32[]{:S(2)}) collective-permute-start(bf16[576,256]{1,0:T(8,128)(2,1)S(1)} %get-tuple-element.16), channel_id=1, source_target_pairs={{0,256},{128,384},{256,0},{384,128},{1,257},{129,385},{257,1},{385... | collective-permute-start | bytes 884744 | tf_op jit(solution)/shard_map/ppermute | solution.py:24
  137.5 2.2 %collective-permute-done.8 = bf16[576,256]{1,0:T(8,128)(2,1)S(1)} collective-permute-done((bf16[576,256]{1,0:T(8,128)(2,1)S(1)}, bf16[576,256]{1,0:T(8,128)(2,1)S(1)}, u32[]{:S(2)}, u32[]{:S(2)}) %collective-permute-start.8) | collective-permute-done | bytes 294944 | tf_op jit(solution)/shard_map/ppermute | solution.py:24
  139.7 1.4 collective-permute-done.9
  141.1 5.8 %collective-permute-done.10 = bf16[576,256]{1,0:T(8,128)(2,1)S(1)} collective-permute-done((bf16[576,256]{1,0:T(8,128)(2,1)S(1)}, bf16[576,256]{1,0:T(8,128)(2,1)S(1)}, u32[]{:S(2)}, u32[]{:S(2)}) %collective-permute-start.10) | collective-permute-done | bytes 294944 | tf_op jit(solution)/shard_map/ppermute | solution.py:24
  147.1 1.9 %collective-permute-start.16 = (bf16[576,256]{1,0:T(8,128)(2,1)S(1)}, bf16[576,256]{1,0:T(8,128)(2,1)S(1)}, u32[]{:S(2)}, u32[]{:S(2)}) collective-permute-start(bf16[576,256]{1,0:T(8,128)(2,1)S(1)} %fusion.4.a0m), channel_id=1, source_target_pairs={{0,64},{64,0},{1,65},{65,1},{2,66},{66,2},{3,67},{67,3},{4,68},{68... | collective-permute-start | bytes 884744 | tf_op jit(solution)/shard_map/ppermute | solution.py:24
  149.1 3.2 %collective-permute-start.14 = (bf16[576,256]{1,0:T(8,128)(2,1)S(1)}, bf16[576,256]{1,0:T(8,128)(2,1)S(1)}, u32[]{:S(2)}, u32[]{:S(2)}) collective-permute-start(bf16[576,256]{1,0:T(8,128)(2,1)S(1)} %fusion.4.a0m), channel_id=1, source_target_pairs={{0,256},{128,384},{256,0},{384,128},{1,257},{129,385},{257,1},{385... | collective-permute-start | bytes 884744 | tf_op jit(solution)/shard_map/ppermute | solution.py:24
  152.3 2.1 %collective-permute-start.12 = (bf16[576,256]{1,0:T(8,128)(2,1)S(1)}, bf16[576,256]{1,0:T(8,128)(2,1)S(1)}, u32[]{:S(2)}, u32[]{:S(2)}) collective-permute-start(bf16[576,256]{1,0:T(8,128)(2,1)S(1)} %fusion.4.a0m), channel_id=1, source_target_pairs={{0,384},{128,0},{256,128},{384,256},{1,385},{129,1},{257,129},{385... | collective-permute-start | bytes 884744 | tf_op jit(solution)/shard_map/ppermute | solution.py:24
  154.3 4.0 %collective-permute-start.11 = (bf16[576,256]{1,0:T(8,128)(2,1)S(1)}, bf16[576,256]{1,0:T(8,128)(2,1)S(1)}, u32[]{:S(2)}, u32[]{:S(2)}) collective-permute-start(bf16[576,256]{1,0:T(8,128)(2,1)S(1)} %fusion.4.a0m), channel_id=1, source_target_pairs={{0,32},{32,0},{1,33},{33,1},{2,34},{34,2},{3,35},{35,3},{4,36},{36... | collective-permute-start | bytes 884744 | tf_op jit(solution)/shard_map/ppermute | solution.py:24
  158.4 2.0 %collective-permute-start.17 = (bf16[576,256]{1,0:T(8,128)(2,1)S(1)}, bf16[576,256]{1,0:T(8,128)(2,1)S(1)}, u32[]{:S(2)}, u32[]{:S(2)}) collective-permute-start(bf16[576,256]{1,0:T(8,128)(2,1)S(1)} %collective-permute-done.16.a3m), channel_id=1, source_target_pairs={{0,32},{32,0},{1,33},{33,1},{2,34},{34,2},{3,35},{35,3},{4,36},{36... | collective-permute-start | bytes 884744 | tf_op jit(solution)/shard_map/ppermute | solution.py:24
  160.4 3.4 %collective-permute-start.15 = (bf16[576,256]{1,0:T(8,128)(2,1)S(1)}, bf16[576,256]{1,0:T(8,128)(2,1)S(1)}, u32[]{:S(2)}, u32[]{:S(2)}) collective-permute-start(bf16[576,256]{1,0:T(8,128)(2,1)S(1)} %collective-permute-done.14.a2m), channel_id=1, source_target_pairs={{0,32},{32,0},{1,33},{33,1},{2,34},{34,2},{3,35},{35,3},{4,36},{36... | collective-permute-start | bytes 884744 | tf_op jit(solution)/shard_map/ppermute | solution.py:24
  164.5 3.7 %collective-permute-start.13 = (bf16[576,256]{1,0:T(8,128)(2,1)S(1)}, bf16[576,256]{1,0:T(8,128)(2,1)S(1)}, u32[]{:S(2)}, u32[]{:S(2)}) collective-permute-start(bf16[576,256]{1,0:T(8,128)(2,1)S(1)} %collective-permute-done.12.a1m), channel_id=1, source_target_pairs={{0,32},{32,0},{1,33},{33,1},{2,34},{34,2},{3,35},{35,3},{4,36},{36... | collective-permute-start | bytes 884744 | tf_op jit(solution)/shard_map/ppermute | solution.py:24
  169.4 1.9 %shard_map.19 = (f32[576,256]{1,0:T(8,128)S(1)}, bf16[576,256]{1,0:T(8,128)(2,1)S(1)}, bf16[576,256]{1,0:T(8,128)(2,1)S(1)}, bf16[576,256]{1,0:T(8,128)(2,1)S(1)}) custom-call(s32[2]{0:T(128)S(1)} %pad_add_fusion.flag, bf16[32,144,128]{2,1,0:T(8,128)(2,1)S(1)} %all_to_all.11.gm, bf16[32,144,128]{2,1,0:T(8,128)(2,1)S(1)} %collective-permute-done.6.go, ...), custom_call_target="tpu_custom_call" | custom-call | flops 1207959552 | bytes 6193160 | tf_op jit(solution)/shard_map/pallas_call | solution.py:93
  171.3 2.9 %collective-permute-start.18 = (bf16[576,256]{1,0:T(8,128)(2,1)S(1)}, bf16[576,256]{1,0:T(8,128)(2,1)S(1)}, u32[]{:S(2)}, u32[]{:S(2)}) collective-permute-start(bf16[576,256]{1,0:T(8,128)(2,1)S(1)} %get-tuple-element.18), channel_id=1, source_target_pairs={{0,128},{128,256},{256,384},{384,0},{1,129},{129,257},{257,385},{3... | collective-permute-start | bytes 884744 | tf_op jit(solution)/shard_map/ppermute | solution.py:24
  174.2 2.2 %collective-permute-start.19 = (bf16[576,256]{1,0:T(8,128)(2,1)S(1)}, bf16[576,256]{1,0:T(8,128)(2,1)S(1)}, u32[]{:S(2)}, u32[]{:S(2)}) collective-permute-start(bf16[576,256]{1,0:T(8,128)(2,1)S(1)} %get-tuple-element.19), channel_id=1, source_target_pairs={{0,64},{64,0},{1,65},{65,1},{2,66},{66,2},{3,67},{67,3},{4,68},{68... | collective-permute-start | bytes 884744 | tf_op jit(solution)/shard_map/ppermute | solution.py:24
  176.5 4.5 %collective-permute-start.20 = (bf16[576,256]{1,0:T(8,128)(2,1)S(1)}, bf16[576,256]{1,0:T(8,128)(2,1)S(1)}, u32[]{:S(2)}, u32[]{:S(2)}) collective-permute-start(bf16[576,256]{1,0:T(8,128)(2,1)S(1)} %get-tuple-element.20), channel_id=1, source_target_pairs={{0,256},{128,384},{256,0},{384,128},{1,257},{129,385},{257,1},{385... | collective-permute-start | bytes 884744 | tf_op jit(solution)/shard_map/ppermute | solution.py:24
  181.0 1.7 collective-permute-done.18
  184.0 5.8 %collective-permute-done.20 = bf16[576,256]{1,0:T(8,128)(2,1)S(1)} collective-permute-done((bf16[576,256]{1,0:T(8,128)(2,1)S(1)}, bf16[576,256]{1,0:T(8,128)(2,1)S(1)}, u32[]{:S(2)}, u32[]{:S(2)}) %collective-permute-start.20) | collective-permute-done | bytes 294944 | tf_op jit(solution)/shard_map/ppermute | solution.py:24
  (24 shorter events, 6.9 us)
Async XLA Ops:
  0.0 14.9 %collective-permute-start.4 = (bf16[576,256]{1,0:T(8,128)(2,1)}, bf16[576,256]{1,0:T(8,128)(2,1)S(1)}, u32[]{:S(2)}, u32[]{:S(2)}) collective-permute-start(bf16[576,256]{1,0:T(8,128)(2,1)} %bitcast.7), channel_id=1, source_target_pairs={{0,64},{64,0},{1,65},{65,1},{2,66},{66,2},{3,67},{67,3},{4,68},{68... | collective-permute-start | bytes 884744 | tf_op jit(solution)/shard_map/ppermute | solution.py:24
  4.0 13.6 %collective-permute-start.2 = (bf16[576,256]{1,0:T(8,128)(2,1)}, bf16[576,256]{1,0:T(8,128)(2,1)S(1)}, u32[]{:S(2)}, u32[]{:S(2)}) collective-permute-start(bf16[576,256]{1,0:T(8,128)(2,1)} %bitcast.8), channel_id=1, source_target_pairs={{0,256},{128,384},{256,0},{384,128},{1,257},{129,385},{257,1},{385... | collective-permute-start | bytes 884744 | tf_op jit(solution)/shard_map/ppermute | solution.py:24
  8.7 13.4 %collective-permute-start.1 = (bf16[576,256]{1,0:T(8,128)(2,1)}, bf16[576,256]{1,0:T(8,128)(2,1)S(1)}, u32[]{:S(2)}, u32[]{:S(2)}) collective-permute-start(bf16[576,256]{1,0:T(8,128)(2,1)} %bitcast.9), channel_id=1, source_target_pairs={{0,384},{128,0},{256,128},{384,256},{1,385},{129,1},{257,129},{385... | collective-permute-start | bytes 884744 | tf_op jit(solution)/shard_map/ppermute | solution.py:24
  11.5 10.6 %collective-permute-start = (bf16[576,256]{1,0:T(8,128)(2,1)}, bf16[576,256]{1,0:T(8,128)(2,1)S(1)}, u32[]{:S(2)}, u32[]{:S(2)}) collective-permute-start(bf16[576,256]{1,0:T(8,128)(2,1)} %bitcast.10), channel_id=1, source_target_pairs={{0,32},{32,0},{1,33},{33,1},{2,34},{34,2},{3,35},{35,3},{4,36},{36... | collective-permute-start | bytes 884744 | tf_op jit(solution)/shard_map/ppermute | solution.py:24
  14.9 7.2 %collective-permute-start.5 = (bf16[576,256]{1,0:T(8,128)(2,1)S(1)}, bf16[576,256]{1,0:T(8,128)(2,1)S(1)}, u32[]{:S(2)}, u32[]{:S(2)}) collective-permute-start(bf16[576,256]{1,0:T(8,128)(2,1)S(1)} %collective-permute-done.4.a3m), channel_id=1, source_target_pairs={{0,32},{32,0},{1,33},{33,1},{2,34},{34,2},{3,35},{35,3},{4,36},{36... | collective-permute-start | bytes 884744 | tf_op jit(solution)/shard_map/ppermute | solution.py:24
  17.6 4.6 %collective-permute-start.3 = (bf16[576,256]{1,0:T(8,128)(2,1)S(1)}, bf16[576,256]{1,0:T(8,128)(2,1)S(1)}, u32[]{:S(2)}, u32[]{:S(2)}) collective-permute-start(bf16[576,256]{1,0:T(8,128)(2,1)S(1)} %collective-permute-done.2.a2m), channel_id=1, source_target_pairs={{0,32},{32,0},{1,33},{33,1},{2,34},{34,2},{3,35},{35,3},{4,36},{36... | collective-permute-start | bytes 884744 | tf_op jit(solution)/shard_map/ppermute | solution.py:24
  22.2 1.0 copy-start
  69.3 52.7 %copy-start.1 = (bf16[256,576]{0,1:T(8,128)(2,1)S(1)}, bf16[256,576]{0,1:T(8,128)(2,1)}, u32[]{:S(2)}) copy-start(bf16[256,576]{0,1:T(8,128)(2,1)} %param.1) | copy-start | bytes 884740
  113.9 8.1 %collective-permute-start.6 = (bf16[32,144,128]{2,1,0:T(8,128)(2,1)S(1)}, bf16[32,144,128]{2,1,0:T(8,128)(2,1)S(1)}, u32[]{:S(2)}, u32[]{:S(2)}) collective-permute-start(bf16[32,144,128]{2,1,0:T(8,128)(2,1)S(1)} %all_to_all.11.gm), channel_id=1, source_target_pairs={{0,32},{32,0},{1,33},{33,1},{2,34},{34,2},{3,35},{35,3},{4,36},{36... | collective-permute-start | bytes 3538952 | tf_op jit(solution)/shard_map/ppermute | solution.py:24
  118.5 3.5 %collective-permute-start.7 = (bf16[576,256]{1,0:T(8,128)(2,1)S(1)}, bf16[576,256]{1,0:T(8,128)(2,1)S(1)}, u32[]{:S(2)}, u32[]{:S(2)}) collective-permute-start(bf16[576,256]{1,0:T(8,128)(2,1)S(1)} %collective-permute-done.1.a1m), channel_id=1, source_target_pairs={{0,32},{32,0},{1,33},{33,1},{2,34},{34,2},{3,35},{35,3},{4,36},{36... | collective-permute-start | bytes 884744 | tf_op jit(solution)/shard_map/ppermute | solution.py:24
  123.9 15.8 %collective-permute-start.8 = (bf16[576,256]{1,0:T(8,128)(2,1)S(1)}, bf16[576,256]{1,0:T(8,128)(2,1)S(1)}, u32[]{:S(2)}, u32[]{:S(2)}) collective-permute-start(bf16[576,256]{1,0:T(8,128)(2,1)S(1)} %get-tuple-element.14), channel_id=1, source_target_pairs={{0,128},{128,256},{256,384},{384,0},{1,129},{129,257},{257,385},{3... | collective-permute-start | bytes 884744 | tf_op jit(solution)/shard_map/ppermute | solution.py:24
  131.0 10.1 %collective-permute-start.9 = (bf16[576,256]{1,0:T(8,128)(2,1)S(1)}, bf16[576,256]{1,0:T(8,128)(2,1)S(1)}, u32[]{:S(2)}, u32[]{:S(2)}) collective-permute-start(bf16[576,256]{1,0:T(8,128)(2,1)S(1)} %get-tuple-element.15), channel_id=1, source_target_pairs={{0,64},{64,0},{1,65},{65,1},{2,66},{66,2},{3,67},{67,3},{4,68},{68... | collective-permute-start | bytes 884744 | tf_op jit(solution)/shard_map/ppermute | solution.py:24
  133.0 14.0 %collective-permute-start.10 = (bf16[576,256]{1,0:T(8,128)(2,1)S(1)}, bf16[576,256]{1,0:T(8,128)(2,1)S(1)}, u32[]{:S(2)}, u32[]{:S(2)}) collective-permute-start(bf16[576,256]{1,0:T(8,128)(2,1)S(1)} %get-tuple-element.16), channel_id=1, source_target_pairs={{0,256},{128,384},{256,0},{384,128},{1,257},{129,385},{257,1},{385... | collective-permute-start | bytes 884744 | tf_op jit(solution)/shard_map/ppermute | solution.py:24
  147.1 11.2 %collective-permute-start.16 = (bf16[576,256]{1,0:T(8,128)(2,1)S(1)}, bf16[576,256]{1,0:T(8,128)(2,1)S(1)}, u32[]{:S(2)}, u32[]{:S(2)}) collective-permute-start(bf16[576,256]{1,0:T(8,128)(2,1)S(1)} %fusion.4.a0m), channel_id=1, source_target_pairs={{0,64},{64,0},{1,65},{65,1},{2,66},{66,2},{3,67},{67,3},{4,68},{68... | collective-permute-start | bytes 884744 | tf_op jit(solution)/shard_map/ppermute | solution.py:24
  149.1 11.3 %collective-permute-start.14 = (bf16[576,256]{1,0:T(8,128)(2,1)S(1)}, bf16[576,256]{1,0:T(8,128)(2,1)S(1)}, u32[]{:S(2)}, u32[]{:S(2)}) collective-permute-start(bf16[576,256]{1,0:T(8,128)(2,1)S(1)} %fusion.4.a0m), channel_id=1, source_target_pairs={{0,256},{128,384},{256,0},{384,128},{1,257},{129,385},{257,1},{385... | collective-permute-start | bytes 884744 | tf_op jit(solution)/shard_map/ppermute | solution.py:24
  152.3 12.2 %collective-permute-start.12 = (bf16[576,256]{1,0:T(8,128)(2,1)S(1)}, bf16[576,256]{1,0:T(8,128)(2,1)S(1)}, u32[]{:S(2)}, u32[]{:S(2)}) collective-permute-start(bf16[576,256]{1,0:T(8,128)(2,1)S(1)} %fusion.4.a0m), channel_id=1, source_target_pairs={{0,384},{128,0},{256,128},{384,256},{1,385},{129,1},{257,129},{385... | collective-permute-start | bytes 884744 | tf_op jit(solution)/shard_map/ppermute | solution.py:24
  154.3 13.8 %collective-permute-start.11 = (bf16[576,256]{1,0:T(8,128)(2,1)S(1)}, bf16[576,256]{1,0:T(8,128)(2,1)S(1)}, u32[]{:S(2)}, u32[]{:S(2)}) collective-permute-start(bf16[576,256]{1,0:T(8,128)(2,1)S(1)} %fusion.4.a0m), channel_id=1, source_target_pairs={{0,32},{32,0},{1,33},{33,1},{2,34},{34,2},{3,35},{35,3},{4,36},{36... | collective-permute-start | bytes 884744 | tf_op jit(solution)/shard_map/ppermute | solution.py:24
  158.4 9.8 %collective-permute-start.17 = (bf16[576,256]{1,0:T(8,128)(2,1)S(1)}, bf16[576,256]{1,0:T(8,128)(2,1)S(1)}, u32[]{:S(2)}, u32[]{:S(2)}) collective-permute-start(bf16[576,256]{1,0:T(8,128)(2,1)S(1)} %collective-permute-done.16.a3m), channel_id=1, source_target_pairs={{0,32},{32,0},{1,33},{33,1},{2,34},{34,2},{3,35},{35,3},{4,36},{36... | collective-permute-start | bytes 884744 | tf_op jit(solution)/shard_map/ppermute | solution.py:24
  160.4 7.8 %collective-permute-start.15 = (bf16[576,256]{1,0:T(8,128)(2,1)S(1)}, bf16[576,256]{1,0:T(8,128)(2,1)S(1)}, u32[]{:S(2)}, u32[]{:S(2)}) collective-permute-start(bf16[576,256]{1,0:T(8,128)(2,1)S(1)} %collective-permute-done.14.a2m), channel_id=1, source_target_pairs={{0,32},{32,0},{1,33},{33,1},{2,34},{34,2},{3,35},{35,3},{4,36},{36... | collective-permute-start | bytes 884744 | tf_op jit(solution)/shard_map/ppermute | solution.py:24
  164.5 4.9 %collective-permute-start.13 = (bf16[576,256]{1,0:T(8,128)(2,1)S(1)}, bf16[576,256]{1,0:T(8,128)(2,1)S(1)}, u32[]{:S(2)}, u32[]{:S(2)}) collective-permute-start(bf16[576,256]{1,0:T(8,128)(2,1)S(1)} %collective-permute-done.12.a1m), channel_id=1, source_target_pairs={{0,32},{32,0},{1,33},{33,1},{2,34},{34,2},{3,35},{35,3},{4,36},{36... | collective-permute-start | bytes 884744 | tf_op jit(solution)/shard_map/ppermute | solution.py:24
  171.3 11.3 %collective-permute-start.18 = (bf16[576,256]{1,0:T(8,128)(2,1)S(1)}, bf16[576,256]{1,0:T(8,128)(2,1)S(1)}, u32[]{:S(2)}, u32[]{:S(2)}) collective-permute-start(bf16[576,256]{1,0:T(8,128)(2,1)S(1)} %get-tuple-element.18), channel_id=1, source_target_pairs={{0,128},{128,256},{256,384},{384,0},{1,129},{129,257},{257,385},{3... | collective-permute-start | bytes 884744 | tf_op jit(solution)/shard_map/ppermute | solution.py:24
  174.2 9.8 %collective-permute-start.19 = (bf16[576,256]{1,0:T(8,128)(2,1)S(1)}, bf16[576,256]{1,0:T(8,128)(2,1)S(1)}, u32[]{:S(2)}, u32[]{:S(2)}) collective-permute-start(bf16[576,256]{1,0:T(8,128)(2,1)S(1)} %get-tuple-element.19), channel_id=1, source_target_pairs={{0,64},{64,0},{1,65},{65,1},{2,66},{66,2},{3,67},{67,3},{4,68},{68... | collective-permute-start | bytes 884744 | tf_op jit(solution)/shard_map/ppermute | solution.py:24
  176.5 13.4 %collective-permute-start.20 = (bf16[576,256]{1,0:T(8,128)(2,1)S(1)}, bf16[576,256]{1,0:T(8,128)(2,1)S(1)}, u32[]{:S(2)}, u32[]{:S(2)}) collective-permute-start(bf16[576,256]{1,0:T(8,128)(2,1)S(1)} %get-tuple-element.20), channel_id=1, source_target_pairs={{0,256},{128,384},{256,0},{384,128},{1,257},{129,385},{257,1},{385... | collective-permute-start | bytes 884744 | tf_op jit(solution)/shard_map/ppermute | solution.py:24
